TPU v7x, 32 devices: a whole 2x2x4 slice. The times are simulated.
32 devices in a mesh: ra: 8 (over z, core), dec: 2 (over y), freq: 2 (over x).
Axes of the slice: x: 2, y: 2, z: 4, core: 2. Of those that a mesh axis runs over, the one named last changes fastest.
Arguments:
- tokens: bfloat16 [64, 32, 64, 192], P('ra', 'dec', 'freq'), may hold values from -12 to 12
- attn_gain: float32 [2, 192], replicated, may hold values from 0.1 to 1.9
- qkv_weight: bfloat16 [2, 192, 576], replicated, may hold values from -3 to 3
- out_weight: bfloat16 [2, 192, 192], replicated, may hold values from -0.4375 to 0.4375
- mlp_gain: float32 [2, 192], replicated, may hold values from 0.1 to 1.9
- up_weight: bfloat16 [2, 192, 768], replicated, may hold values from -0.4375 to 0.4375
- down_weight: bfloat16 [2, 768, 192], replicated, may hold values from -0.21875 to 0.21875
- merge_gain: float32 [1536], replicated, may hold values from 0.1 to 1.9
- merge_weight: bfloat16 [1536, 384], replicated, may hold values from -0.15625 to 0.15625
Outputs:
- merged: bfloat16 [32, 16, 32, 384], P('ra', 'dec', 'freq')
All inputs are finite; a program needn't handle non-finite values.
Results may differ from a plain program's by a relative error of at most 0.023.
Values may be sent and summed in bfloat16 or wider, within the bound.
No kernel may reach another device: no remote copies, remote signals or barrier semaphores. Data moves between devices by JAX's collectives and lax.ppermute only.
A program may use at most 64 MiB of HBM per device.

v0:
```python
import jax
import jax.numpy as jnp
from jax import lax
from jax.sharding import PartitionSpec as P

HEADS = 6
WIN = 8


def shifted_2(value, axis, steps):
    count = lax.axis_size(axis)
    pairs = [(source, (source + steps) % count) for source in range(count)]
    return lax.ppermute(value, axis, pairs)


def layer_norm(values, norm_gain):
    row_mean = jnp.mean(values, axis=-1, keepdims=True)
    centred = values - row_mean
    row_var = jnp.mean(centred * centred, axis=-1, keepdims=True)
    return centred * lax.rsqrt(row_var + 1e-05) * norm_gain


def to_windows(volume):
    rows_ra, rows_dec, rows_freq, depth = volume.shape
    blocked = volume.reshape(
        rows_ra // WIN, WIN, rows_dec // WIN, WIN, rows_freq // WIN, WIN, depth
    )
    return blocked.transpose(0, 2, 4, 1, 3, 5, 6).reshape(-1, WIN * WIN * WIN, depth)


def from_windows(windows, rows_ra, rows_dec, rows_freq):
    depth = windows.shape[-1]
    blocked = windows.reshape(
        rows_ra // WIN, rows_dec // WIN, rows_freq // WIN, WIN, WIN, WIN, depth
    )
    return blocked.transpose(0, 3, 1, 4, 2, 5, 6).reshape(rows_ra, rows_dec, rows_freq, depth)


def window_block(window, labels, layer_params):
    attn_norm, qkv_mat, out_mat, mlp_norm, up_mat, down_mat = layer_params
    model_width = window.shape[-1]
    head_size = model_width // HEADS
    normed = layer_norm(window.astype(jnp.float32), attn_norm).astype(jnp.bfloat16)
    projected = jnp.dot(normed, qkv_mat, preferred_element_type=jnp.float32).astype(jnp.bfloat16)
    split_heads = projected.reshape(-1, 3, HEADS, head_size)
    scores = jnp.einsum(
        "qhd,khd->hqk", split_heads[:, 0], split_heads[:, 1], preferred_element_type=jnp.float32
    ) * head_size ** (-0.5)
    if labels is not None:
        allowed = labels[:, None] == labels[None, :]
        scores = jnp.where(allowed[None], scores, -1e30)
    row_top = jnp.max(scores, axis=-1, keepdims=True)
    exponent = jnp.exp(scores - row_top)
    weights_bf = (exponent / jnp.sum(exponent, axis=-1, keepdims=True)).astype(jnp.bfloat16)
    attended = jnp.einsum(
        "hqk,khd->qhd", weights_bf, split_heads[:, 2], preferred_element_type=jnp.float32
    )
    attended = attended.astype(jnp.bfloat16).reshape(-1, model_width)
    resid = (
        window.astype(jnp.float32) + jnp.dot(attended, out_mat, preferred_element_type=jnp.float32)
    ).astype(jnp.bfloat16)
    normed_two = layer_norm(resid.astype(jnp.float32), mlp_norm).astype(jnp.bfloat16)
    activ = jax.nn.gelu(
        jnp.dot(normed_two, up_mat, preferred_element_type=jnp.float32), approximate=False
    ).astype(jnp.bfloat16)
    return (
        resid.astype(jnp.float32) + jnp.dot(activ, down_mat, preferred_element_type=jnp.float32)
    ).astype(jnp.bfloat16)


def run_block(volume, layer_params, label_grid):
    rows_ra, rows_dec, rows_freq, depth = volume.shape
    windows = to_windows(volume)
    if label_grid is None:
        outputs = lax.map(lambda window: window_block(window, None, layer_params), windows)
    else:
        label_windows = to_windows(label_grid[..., None])[..., 0]
        outputs = lax.map(
            lambda window_pair: window_block(window_pair[0], window_pair[1], layer_params),
            (windows, label_windows),
        )
    return from_windows(outputs, rows_ra, rows_dec, rows_freq)


def region(coord, total):
    return jnp.where(coord < total - WIN, 0, jnp.where(coord < total - WIN // 2, 1, 2)).astype(
        jnp.int32
    )


def region_labels(coord_ra, coord_dec, coord_freq, total_ra, total_dec, total_freq):
    label_ra = region(coord_ra, total_ra)[:, None, None]
    label_dec = region(coord_dec, total_dec)[None, :, None]
    label_freq = region(coord_freq, total_freq)[None, None, :]
    return label_ra * 9 + label_dec * 3 + label_freq


def merge_patches(volume, merge_gain, merge_weight):
    rows_ra, rows_dec, rows_freq, depth = volume.shape
    grouped = volume.reshape(rows_ra // 2, 2, rows_dec // 2, 2, rows_freq // 2, 2, depth)
    grouped = grouped.transpose(0, 2, 4, 1, 3, 5, 6).reshape(
        rows_ra // 2, rows_dec // 2, rows_freq // 2, 8 * depth
    )
    normed = layer_norm(grouped.astype(jnp.float32), merge_gain).astype(jnp.bfloat16)
    return jnp.dot(normed, merge_weight, preferred_element_type=jnp.float32).astype(jnp.bfloat16)


def pick_layer(layer_index, attn_gain, qkv_weight, out_weight, mlp_gain, up_weight, down_weight):
    return (
        attn_gain[layer_index],
        qkv_weight[layer_index],
        out_weight[layer_index],
        mlp_gain[layer_index],
        up_weight[layer_index],
        down_weight[layer_index],
    )


def on_device(
    tokens,
    attn_gain,
    qkv_weight,
    out_weight,
    mlp_gain,
    up_weight,
    down_weight,
    merge_gain,
    merge_weight,
):
    rows_ra, rows_dec, rows_freq, depth = tokens.shape
    half_win = WIN // 2
    first_out = run_block(
        tokens,
        pick_layer(0, attn_gain, qkv_weight, out_weight, mlp_gain, up_weight, down_weight),
        None,
    )
    incoming = shifted_2(first_out[:half_win], "ra", -1)
    shifted = jnp.concatenate([first_out[half_win:], incoming], axis=0)
    incoming = shifted_2(shifted[:, :half_win], "dec", -1)
    shifted = jnp.concatenate([shifted[:, half_win:], incoming], axis=1)
    incoming = shifted_2(shifted[:, :, :half_win], "freq", -1)
    shifted = jnp.concatenate([shifted[:, :, half_win:], incoming], axis=2)
    coord_ra = lax.axis_index("ra") * rows_ra + jnp.arange(rows_ra, dtype=jnp.int32)
    coord_dec = lax.axis_index("dec") * rows_dec + jnp.arange(rows_dec, dtype=jnp.int32)
    coord_freq = lax.axis_index("freq") * rows_freq + jnp.arange(rows_freq, dtype=jnp.int32)
    label_grid = region_labels(
        coord_ra,
        coord_dec,
        coord_freq,
        rows_ra * lax.axis_size("ra"),
        rows_dec * lax.axis_size("dec"),
        rows_freq * lax.axis_size("freq"),
    )
    second_out = run_block(
        shifted,
        pick_layer(1, attn_gain, qkv_weight, out_weight, mlp_gain, up_weight, down_weight),
        label_grid,
    )
    incoming = shifted_2(second_out[-half_win:], "ra", 1)
    restored = jnp.concatenate([incoming, second_out[:-half_win]], axis=0)
    incoming = shifted_2(restored[:, -half_win:], "dec", 1)
    restored = jnp.concatenate([incoming, restored[:, :-half_win]], axis=1)
    incoming = shifted_2(restored[:, :, -half_win:], "freq", 1)
    restored = jnp.concatenate([incoming, restored[:, :, :-half_win]], axis=2)
    return merge_patches(restored, merge_gain, merge_weight)


def solution(mesh):
    placed = (P("ra", "dec", "freq", None), P(), P(), P(), P(), P(), P(), P(), P())
    return jax.shard_map(
        on_device,
        mesh=mesh,
        in_specs=placed,
        out_specs=P("ra", "dec", "freq", None),
        check_vma=False,
    )
```

profile of v0, /device:TPU:0, one launch (start us, length us, event | category | flops | bytes accessed | tf_op | source)
XLA Modules:
  0.0 410.2 jit_solution(10040637311794162074)
XLA Ops:
  14.8 131.7 %while.20 = (s32[]{:T(128)}, bf16[8,512,192]{1,2,0:T(8,128)(2,1)}, bf16[8,512,192]{1,2,0:T(8,128)(2,1)S(1)}, f32[1,192]{1,0:T(1,128)S(1)}, bf16[192,576]{1,0:T(8...) while((s32[]{:T(128)}, bf16[8,512,192]{1,2,0:T(8,128)(2,1)}, ...), condition=%wide.region_7.8_spmd, body=%wide.region_0.7_spmd.sunk | while | flops 690587136 | bytes 17758836 | solution.py:75
  25.5 5.8 %fusion.277 = bf16[8,512,192]{1,2,0:T(8,128)(2,1)} fusion(bf16[8,512,192]{1,2,0:T(8,128)(2,1)} %get-tuple-element.351, s32[]{:T(128)} %get-tuple-element.350, f32[512,192]{0,1:T(8,128)S(1)} %get-tuple-element.324, bf16[768,192]{1,0:T(8,128)(2,1)} %get-tuple-element.368, bf16[192,768]{1,0:T(8,128)(2,1)} %get-tuple-element.367, f32[192]{0:T(256)S(1)} %bitcast.250, ...), kind=kOutput, calls=%fused_computation.35.clone.1 | convolution fusion | flops 328138752 | bytes 1676800 | tf_op jit(solution)/shard_map/while/body/eval_jaxpr/dot_general | solution.py:67
  74.9 5.8 %fusion.277 = bf16[8,512,192]{1,2,0:T(8,128)(2,1)} fusion(bf16[8,512,192]{1,2,0:T(8,128)(2,1)} %get-tuple-element.351, s32[]{:T(128)} %get-tuple-element.350, f32[512,192]{0,1:T(8,128)S(1)} %get-tuple-element.324, bf16[768,192]{1,0:T(8,128)(2,1)} %get-tuple-element.368, bf16[192,768]{1,0:T(8,128)(2,1)} %get-tuple-element.367, f32[192]{0:T(256)S(1)} %bitcast.250, ...), kind=kOutput, calls=%fused_computation.35.clone.1 | convolution fusion | flops 328138752 | bytes 1676800 | tf_op jit(solution)/shard_map/while/body/eval_jaxpr/dot_general | solution.py:67
  91.4 5.8 %fusion.277 = bf16[8,512,192]{1,2,0:T(8,128)(2,1)} fusion(bf16[8,512,192]{1,2,0:T(8,128)(2,1)} %get-tuple-element.351, s32[]{:T(128)} %get-tuple-element.350, f32[512,192]{0,1:T(8,128)S(1)} %get-tuple-element.324, bf16[768,192]{1,0:T(8,128)(2,1)} %get-tuple-element.368, bf16[192,768]{1,0:T(8,128)(2,1)} %get-tuple-element.367, f32[192]{0:T(256)S(1)} %bitcast.250, ...), kind=kOutput, calls=%fused_computation.35.clone.1 | convolution fusion | flops 328138752 | bytes 1676800 | tf_op jit(solution)/shard_map/while/body/eval_jaxpr/dot_general | solution.py:67
  107.8 5.8 %fusion.277 = bf16[8,512,192]{1,2,0:T(8,128)(2,1)} fusion(bf16[8,512,192]{1,2,0:T(8,128)(2,1)} %get-tuple-element.351, s32[]{:T(128)} %get-tuple-element.350, f32[512,192]{0,1:T(8,128)S(1)} %get-tuple-element.324, bf16[768,192]{1,0:T(8,128)(2,1)} %get-tuple-element.368, bf16[192,768]{1,0:T(8,128)(2,1)} %get-tuple-element.367, f32[192]{0:T(256)S(1)} %bitcast.250, ...), kind=kOutput, calls=%fused_computation.35.clone.1 | convolution fusion | flops 328138752 | bytes 1676800 | tf_op jit(solution)/shard_map/while/body/eval_jaxpr/dot_general | solution.py:67
  157.5 11.2 %collective-permute-done = bf16[4,16,32,192]{3,2,1,0:T(8,128)(2,1)S(1)} collective-permute-done((bf16[4,16,32,192]{3,2,1,0:T(8,128)(2,1)}, bf16[4,16,32,192]{3,2,1,0:T(8,128)(2,1)S(1)}, u32[]{:S(2)}, u32[]{:S(2)}) %collective-permute-start) | collective-permute-done | bytes 786464 | tf_op jit(solution)/shard_map/ppermute | solution.py:13
  172.1 9.3 %collective-permute-done.1 = bf16[8,4,32,192]{3,2,1,0:T(8,128)(2,1)S(1)} collective-permute-done((bf16[8,4,32,192]{3,2,1,0:T(8,128)(2,1)S(1)}, bf16[8,4,32,192]{3,2,1,0:T(8,128)(2,1)S(1)}, u32[]{:S(2)}, u32[]{:S(2)}) %collective-permute-start.1) | collective-permute-done | bytes 393248 | tf_op jit(solution)/shard_map/ppermute | solution.py:13
  197.4 144.7 %while.21 = (s32[]{:T(128)}, bf16[8,512,192]{1,2,0:T(8,128)(2,1)}, bf16[8,512,192]{1,2,0:T(8,128)(2,1)S(1)}, f32[1,192]{1,0:T(1,128)S(1)}, bf16[192,576]{1,0:T(8...) while((s32[]{:T(128)}, bf16[8,512,192]{1,2,0:T(8,128)(2,1)}, ...), condition=%wide.region_15.16_spmd, body=%wide.region_8.15_spmd.sunk | while | flops 692422144 | bytes 18293376 | solution.py:78
  199.9 6.0 %fusion.285 = (f32[6,512]{1,0:T(8,128)S(1)}, f32[6,512,512]{1,2,0:T(8,128)}) fusion(pred[512,512]{0,1:T(8,128)(4,1)} %broadcast_compare_fusion.2, bf16[512,3,6,32]{0,3,2,1:T(8,128)(2,1)S(1)} %bitcast.229), kind=kOutput, calls=%fused_computation.297.clone.1 | convolution fusion | flops 106955264 | bytes 6959104 | tf_op jit(solution)/shard_map/while/body/eval_jaxpr/sub | solution.py:53
  209.7 5.8 %fusion.288 = bf16[8,512,192]{1,2,0:T(8,128)(2,1)} fusion(bf16[8,512,192]{1,2,0:T(8,128)(2,1)} %get-tuple-element.382, s32[]{:T(128)} %get-tuple-element.381, f32[512,192]{0,1:T(8,128)S(1)} %get-tuple-element.338, bf16[768,192]{1,0:T(8,128)(2,1)} %get-tuple-element.401, bf16[192,768]{1,0:T(8,128)(2,1)} %get-tuple-element.400, ...), kind=kOutput, calls=%fused_computation.161.clone.1 | convolution fusion | flops 328138752 | bytes 1676800 | tf_op jit(solution)/shard_map/while/body/eval_jaxpr/dot_general | solution.py:67
  218.0 6.0 %fusion.285 = (f32[6,512]{1,0:T(8,128)S(1)}, f32[6,512,512]{1,2,0:T(8,128)}) fusion(pred[512,512]{0,1:T(8,128)(4,1)} %broadcast_compare_fusion.2, bf16[512,3,6,32]{0,3,2,1:T(8,128)(2,1)S(1)} %bitcast.229), kind=kOutput, calls=%fused_computation.297.clone.1 | convolution fusion | flops 106955264 | bytes 6959104 | tf_op jit(solution)/shard_map/while/body/eval_jaxpr/sub | solution.py:53
  236.0 6.0 %fusion.285 = (f32[6,512]{1,0:T(8,128)S(1)}, f32[6,512,512]{1,2,0:T(8,128)}) fusion(pred[512,512]{0,1:T(8,128)(4,1)} %broadcast_compare_fusion.2, bf16[512,3,6,32]{0,3,2,1:T(8,128)(2,1)S(1)} %bitcast.229), kind=kOutput, calls=%fused_computation.297.clone.1 | convolution fusion | flops 106955264 | bytes 6959104 | tf_op jit(solution)/shard_map/while/body/eval_jaxpr/sub | solution.py:53
  254.1 6.0 %fusion.285 = (f32[6,512]{1,0:T(8,128)S(1)}, f32[6,512,512]{1,2,0:T(8,128)}) fusion(pred[512,512]{0,1:T(8,128)(4,1)} %broadcast_compare_fusion.2, bf16[512,3,6,32]{0,3,2,1:T(8,128)(2,1)S(1)} %bitcast.229), kind=kOutput, calls=%fused_computation.297.clone.1 | convolution fusion | flops 106955264 | bytes 6959104 | tf_op jit(solution)/shard_map/while/body/eval_jaxpr/sub | solution.py:53
  263.9 5.8 %fusion.288 = bf16[8,512,192]{1,2,0:T(8,128)(2,1)} fusion(bf16[8,512,192]{1,2,0:T(8,128)(2,1)} %get-tuple-element.382, s32[]{:T(128)} %get-tuple-element.381, f32[512,192]{0,1:T(8,128)S(1)} %get-tuple-element.338, bf16[768,192]{1,0:T(8,128)(2,1)} %get-tuple-element.401, bf16[192,768]{1,0:T(8,128)(2,1)} %get-tuple-element.400, ...), kind=kOutput, calls=%fused_computation.161.clone.1 | convolution fusion | flops 328138752 | bytes 1676800 | tf_op jit(solution)/shard_map/while/body/eval_jaxpr/dot_general | solution.py:67
  272.2 6.0 %fusion.285 = (f32[6,512]{1,0:T(8,128)S(1)}, f32[6,512,512]{1,2,0:T(8,128)}) fusion(pred[512,512]{0,1:T(8,128)(4,1)} %broadcast_compare_fusion.2, bf16[512,3,6,32]{0,3,2,1:T(8,128)(2,1)S(1)} %bitcast.229), kind=kOutput, calls=%fused_computation.297.clone.1 | convolution fusion | flops 106955264 | bytes 6959104 | tf_op jit(solution)/shard_map/while/body/eval_jaxpr/sub | solution.py:53
  282.1 5.8 %fusion.288 = bf16[8,512,192]{1,2,0:T(8,128)(2,1)} fusion(bf16[8,512,192]{1,2,0:T(8,128)(2,1)} %get-tuple-element.382, s32[]{:T(128)} %get-tuple-element.381, f32[512,192]{0,1:T(8,128)S(1)} %get-tuple-element.338, bf16[768,192]{1,0:T(8,128)(2,1)} %get-tuple-element.401, bf16[192,768]{1,0:T(8,128)(2,1)} %get-tuple-element.400, ...), kind=kOutput, calls=%fused_computation.161.clone.1 | convolution fusion | flops 328138752 | bytes 1676800 | tf_op jit(solution)/shard_map/while/body/eval_jaxpr/dot_general | solution.py:67
  290.3 6.0 %fusion.285 = (f32[6,512]{1,0:T(8,128)S(1)}, f32[6,512,512]{1,2,0:T(8,128)}) fusion(pred[512,512]{0,1:T(8,128)(4,1)} %broadcast_compare_fusion.2, bf16[512,3,6,32]{0,3,2,1:T(8,128)(2,1)S(1)} %bitcast.229), kind=kOutput, calls=%fused_computation.297.clone.1 | convolution fusion | flops 106955264 | bytes 6959104 | tf_op jit(solution)/shard_map/while/body/eval_jaxpr/sub | solution.py:53
  300.1 5.8 %fusion.288 = bf16[8,512,192]{1,2,0:T(8,128)(2,1)} fusion(bf16[8,512,192]{1,2,0:T(8,128)(2,1)} %get-tuple-element.382, s32[]{:T(128)} %get-tuple-element.381, f32[512,192]{0,1:T(8,128)S(1)} %get-tuple-element.338, bf16[768,192]{1,0:T(8,128)(2,1)} %get-tuple-element.401, bf16[192,768]{1,0:T(8,128)(2,1)} %get-tuple-element.400, ...), kind=kOutput, calls=%fused_computation.161.clone.1 | convolution fusion | flops 328138752 | bytes 1676800 | tf_op jit(solution)/shard_map/while/body/eval_jaxpr/dot_general | solution.py:67
  308.4 6.0 %fusion.285 = (f32[6,512]{1,0:T(8,128)S(1)}, f32[6,512,512]{1,2,0:T(8,128)}) fusion(pred[512,512]{0,1:T(8,128)(4,1)} %broadcast_compare_fusion.2, bf16[512,3,6,32]{0,3,2,1:T(8,128)(2,1)S(1)} %bitcast.229), kind=kOutput, calls=%fused_computation.297.clone.1 | convolution fusion | flops 106955264 | bytes 6959104 | tf_op jit(solution)/shard_map/while/body/eval_jaxpr/sub | solution.py:53
  326.5 6.0 %fusion.285 = (f32[6,512]{1,0:T(8,128)S(1)}, f32[6,512,512]{1,2,0:T(8,128)}) fusion(pred[512,512]{0,1:T(8,128)(4,1)} %broadcast_compare_fusion.2, bf16[512,3,6,32]{0,3,2,1:T(8,128)(2,1)S(1)} %bitcast.229), kind=kOutput, calls=%fused_computation.297.clone.1 | convolution fusion | flops 106955264 | bytes 6959104 | tf_op jit(solution)/shard_map/while/body/eval_jaxpr/sub | solution.py:53
  345.5 15.9 %collective-permute-done.3 = bf16[4,16,32,192]{3,2,1,0:T(8,128)(2,1)S(1)} collective-permute-done((bf16[4,16,32,192]{3,2,1,0:T(8,128)(2,1)S(1)}, bf16[4,16,32,192]{3,2,1,0:T(8,128)(2,1)S(1)}, u32[]{:S(2)}, u32[]{:S(2)}) %collective-permute-start.3) | collective-permute-done | bytes 786464 | tf_op jit(solution)/shard_map/ppermute | solution.py:13
  363.1 10.6 %collective-permute-done.4 = bf16[8,4,32,192]{3,2,1,0:T(8,128)(2,1)S(1)} collective-permute-done((bf16[8,4,32,192]{3,2,1,0:T(8,128)(2,1)S(1)}, bf16[8,4,32,192]{3,2,1,0:T(8,128)(2,1)S(1)}, u32[]{:S(2)}, u32[]{:S(2)}) %collective-permute-start.4) | collective-permute-done | bytes 393248 | tf_op jit(solution)/shard_map/ppermute | solution.py:13
  383.2 5.8 %reshape.218 = f32[4,2,8,2,16,2,192]{6,5,4,3,2,1,0:T(2,128)} reshape(f32[8,16,32,192]{3,2,1,0:T(8,128)} %fusion.214) | data formatting | bytes 6291456 | tf_op jit(solution)/shard_map/convert_element_type | solution.py:104
  400.3 6.3 %reshape.216 = f32[4,8,16,1536]{3,2,1,0:T(8,128)} reshape(f32[4,8,16,2,2,2,192]{6,5,4,3,2,1,0:T(2,128)} %copy.43) | data formatting | bytes 6291456 | tf_op jit(solution)/shard_map/convert_element_type | solution.py:104
  (261 shorter events, 255.8 us)
Async XLA Ops:
  0.0 406.5 %copy-start = (bf16[1536,384]{1,0:T(8,128)(2,1)S(1)}, bf16[1536,384]{1,0:T(8,128)(2,1)}, u32[]{:S(2)}) copy-start(bf16[1536,384]{1,0:T(8,128)(2,1)} %param.21) | copy-start | bytes 3538948
  2.0 6.9 %copy-start.4 = (bf16[8,16,32,192]{3,2,1,0:T(8,128)(2,1)S(1)}, bf16[8,16,32,192]{3,2,1,0:T(8,128)(2,1)}, u32[]{:S(2)}) copy-start(bf16[8,16,32,192]{3,2,1,0:T(8,128)(2,1)} %param.13) | copy-start | bytes 4718596
  10.6 3.0 copy-start.7
  10.6 3.0 copy-start.8
  151.6 17.1 %collective-permute-start = (bf16[4,16,32,192]{3,2,1,0:T(8,128)(2,1)}, bf16[4,16,32,192]{3,2,1,0:T(8,128)(2,1)S(1)}, u32[]{:S(2)}, u32[]{:S(2)}) collective-permute-start(bf16[4,16,32,192]{3,2,1,0:T(8,128)(2,1)} %bitcast.32), channel_id=1, source_target_pairs={{0,28},{4,0},{8,4},{12,8},{16,12},{20,16},{24,20},{28,24},{1,29},{... | collective-permute-start | bytes 2359304 | tf_op jit(solution)/shard_map/ppermute | solution.py:13
  157.4 13.0 %copy-start.2 = (bf16[1,4,2,8,4,8,192]{6,5,4,3,2,1,0:T(8,128)(2,1)}, bf16[1,4,2,8,4,8,192]{6,5,4,3,2,1,0:T(8,128)(2,1)S(1)}, u32[]{:S(2)}) copy-start(bf16[1,4,2,8,4,8,192]{6,5,4,3,2,1,0:T(8,128)(2,1)S(1)} %copy.35) | copy-start | bytes 2359300
  168.7 1.7 copy-start.3
  168.8 12.6 %collective-permute-start.1 = (bf16[8,4,32,192]{3,2,1,0:T(8,128)(2,1)S(1)}, bf16[8,4,32,192]{3,2,1,0:T(8,128)(2,1)S(1)}, u32[]{:S(2)}, u32[]{:S(2)}) collective-permute-start(bf16[8,4,32,192]{3,2,1,0:T(8,128)(2,1)S(1)} %pad_maximum_fusion.4), channel_id=1, source_target_pairs={{0,2},{2,0},{1,3},{3,1},{4,6},{6,4},{5,7},{7,5},{8,10},{10,8},{9,1... | collective-permute-start | bytes 1179656 | tf_op jit(solution)/shard_map/ppermute | solution.py:13
  181.4 0.8 copy-start.5
  183.0 5.3 %copy-start.6 = (bf16[8,4,32,192]{3,2,1,0:T(8,128)(2,1)S(1)}, bf16[8,4,32,192]{3,2,1,0:T(8,128)(2,1)}, u32[]{:S(2)}) copy-start(bf16[8,4,32,192]{3,2,1,0:T(8,128)(2,1)} %copy-done.5) | copy-start | bytes 1179652
  183.0 6.7 %collective-permute-start.2 = (bf16[8,16,4,192]{3,2,1,0:T(4,128)(2,1)}, bf16[8,16,4,192]{3,2,1,0:T(4,128)(2,1)}, u32[]{:S(2)}, u32[]{:S(2)}) collective-permute-start(bf16[8,16,4,192]{3,2,1,0:T(4,128)(2,1)} %pad_maximum_fusion.6), channel_id=1, source_target_pairs={{0,1},{1,0},{2,3},{3,2},{4,5},{5,4},{6,7},{7,6},{8,9},{9,8},{10,11... | collective-permute-start | bytes 589832 | tf_op jit(solution)/shard_map/ppermute | solution.py:13
  345.1 16.3 %collective-permute-start.3 = (bf16[4,16,32,192]{3,2,1,0:T(8,128)(2,1)S(1)}, bf16[4,16,32,192]{3,2,1,0:T(8,128)(2,1)S(1)}, u32[]{:S(2)}, u32[]{:S(2)}) collective-permute-start(bf16[4,16,32,192]{3,2,1,0:T(8,128)(2,1)S(1)} %bitcast.243), channel_id=1, source_target_pairs={{0,4},{4,8},{8,12},{12,16},{16,20},{20,24},{24,28},{28,0},{1,5},{5... | collective-permute-start | bytes 2359304 | tf_op jit(solution)/shard_map/ppermute | solution.py:13
  361.5 12.2 %collective-permute-start.4 = (bf16[8,4,32,192]{3,2,1,0:T(8,128)(2,1)S(1)}, bf16[8,4,32,192]{3,2,1,0:T(8,128)(2,1)S(1)}, u32[]{:S(2)}, u32[]{:S(2)}) collective-permute-start(bf16[8,4,32,192]{3,2,1,0:T(8,128)(2,1)S(1)} %pad_maximum_fusion.3), channel_id=1, source_target_pairs={{0,2},{2,0},{1,3},{3,1},{4,6},{6,4},{5,7},{7,5},{8,10},{10,8},{9,1... | collective-permute-start | bytes 1179656 | tf_op jit(solution)/shard_map/ppermute | solution.py:13
  373.9 6.4 %collective-permute-start.5 = (bf16[8,16,4,192]{3,2,1,0:T(4,128)(2,1)S(1)}, bf16[8,16,4,192]{3,2,1,0:T(4,128)(2,1)S(1)}, u32[]{:S(2)}, u32[]{:S(2)}) collective-permute-start(bf16[8,16,4,192]{3,2,1,0:T(4,128)(2,1)S(1)} %pad_maximum_fusion.5), channel_id=1, source_target_pairs={{0,1},{1,0},{2,3},{3,2},{4,5},{5,4},{6,7},{7,6},{8,9},{9,8},{10,11... | collective-permute-start | bytes 589832 | tf_op jit(solution)/shard_map/ppermute | solution.py:13
  389.0 4.1 copy-start.1
  400.3 6.3 %copy-start.9 = (f32[1536]{0:T(1024)S(1)}, f32[1536]{0:T(1024)}, u32[]{:S(2)}) copy-start(f32[1536]{0:T(1024)} %param.20) | copy-start | bytes 18436
where the time goes:
time: 412 us; the launch traced here: 410 us
  matrix products  268 us (65%)
  waiting for transfers between devices  52.7 us (13%)
  local copies, waits for them, and re-layouts  49.6 us (12%)
  other arithmetic  27.8 us (7%)
  starting transfers between devices  11 us (3%)
    dot_general x16, matrix products, window_block(): jnp.dot(activ, down_mat, preferred_element_type=jnp.float32)  92.5 us
    sub x16, matrix products, window_block(): exponent = jnp.exp(scores - row_top)  91.2 us
    dot_general x16, matrix products, window_block(): jnp.einsum('hqk,khd->qhd', weights_bf, split_heads[:, 2], preferred_eleme...  54.9 us
    ppermute x6, waiting for transfers between devices, shifted_2(): return lax.ppermute(value, axis, pairs)  52.7 us
    dot_general x16, matrix products, window_block(): jnp.dot(normed, qkv_mat, preferred_element_type=jnp.float32)  21.7 us
    convert_element_type x3, local copies, waits for them, and re-layouts, merge_patches(): grouped.astype(jnp.float32)  15.6 us
    ppermute x6, starting transfers between devices, shifted_2(): return lax.ppermute(value, axis, pairs)  11 us
  transfers between devices with their start and end apart: 6, of which 6 were waited for; matrix products, arithmetic and copies ran while one was open for 2% of the time, Pallas kernels for 0%

commit v1 on v0

v1 whole, which is shorter than its diff:
```python
import functools

import jax
import jax.numpy as jnp
from jax import lax
from jax.experimental import pallas as pl
from jax.experimental.pallas import tpu as pltpu
from jax.sharding import PartitionSpec as P

HEADS = 6
WIN = 8
HALF = WIN // 2
PAIR = 2 * WIN
TOKENS = WIN * WIN * WIN
LOG2E = 1.4426950408889634
SUM_LOW = 2.0**-80
SUM_HIGH = 2.0**100
FAR = -1e30
VMEM_LIMIT = 30 * 2**20
FIRST_LIMIT = 60 * 2**20

f32 = jnp.float32
bf16 = jnp.bfloat16


def dot_f32(a, b):
    return jnp.dot(a, b, preferred_element_type=f32)


def dot_nt(a, b):
    return lax.dot_general(a, b, (((1,), (1,)), ((), ())), preferred_element_type=f32)


def layer_norm(values, gain):
    mean = jnp.mean(values, axis=-1, keepdims=True)
    centred = values - mean
    var = jnp.mean(centred * centred, axis=-1, keepdims=True)
    return centred * lax.rsqrt(var + 1e-05) * gain


def split_mask(rows, width):
    lane = lax.broadcasted_iota(jnp.int32, (rows, 128), 1) - (width - 128)
    row = lax.broadcasted_iota(jnp.int32, (rows, 128), 0)
    late_ra = row // (rows // 2)
    late_dec = (row // (WIN * HALF)) % 2
    late_freq = 1 - (row % WIN) // HALF
    late = jnp.where(lane < 2, late_ra, jnp.where(lane < 4, late_dec, late_freq))
    outside = jnp.where(lane < 0, 1, jnp.where(lane < 6, 0, 1))
    same = jnp.where(lane % 2 == late, 1, 0)
    key_cols = jnp.where(outside + 1 - same == 0, 1.0, 0.0)
    query_cols = jnp.where(outside + same == 0, FAR, 0.0)
    return query_cols.astype(f32), key_cols.astype(f32)


def attention(normed, qkv, width, masks, chunk, safe):
    rows = normed.shape[0]
    head_size = width // HEADS
    projected = dot_f32(normed, qkv)
    q = projected[:, :256] * f32(head_size**-0.5 * LOG2E)
    k = projected[:, 256:512]
    if masks is not None:
        query_cols, key_cols, active = masks
        extra = lax.broadcasted_iota(jnp.int32, (1, 128), 1) >= width - 128
        q = jnp.concatenate(
            [q[:, :128], jnp.where(extra, query_cols * active, q[:, 128:])], axis=1
        )
        k = jnp.concatenate([k[:, :128], jnp.where(extra, key_cols, k[:, 128:])], axis=1)
    q, k, v = q.astype(bf16), k.astype(bf16), projected[:, 512:].astype(bf16)
    ones = jnp.ones((rows, 128), bf16)
    v_low = jnp.concatenate([v[:, :128], ones], axis=1)
    v_high = jnp.concatenate([ones, v[:, 128:]], axis=1)
    lane = lax.broadcasted_iota(jnp.int32, (1, 256), 1)
    low_heads = 128 // head_size
    outs = []
    bad = jnp.zeros((1, 128), f32)
    for start in range(0, rows, chunk):
        q_part = q[start : start + chunk]
        data = [None, None]
        total = [None, None]
        for head in range(HEADS):
            own = (lane >= head_size * head) & (lane < head_size * (head + 1))
            q_head = jnp.where(own | (lane >= width), q_part, jnp.zeros((), bf16))
            scores = dot_nt(q_head, k)
            if safe:
                scores = scores - jnp.max(scores, axis=-1, keepdims=True)
            weights = jnp.exp2(scores).astype(bf16)
            side = 0 if head < low_heads else 1
            both = dot_f32(weights, v_low if side == 0 else v_high)
            mine, other = both[:, :128], both[:, 128:]
            if side:
                mine, other = other, mine
            if data[side] is None:
                data[side], total[side] = mine, other
            else:
                lanes = own[:, 128 * side : 128 * side + 128]
                data[side] = jnp.where(lanes, mine, data[side])
                total[side] = jnp.where(lanes, other, total[side])
        if not safe:
            for t in total:
                fine = jnp.where((t >= SUM_LOW) & (t <= SUM_HIGH), f32(0), f32(1))
                bad = jnp.maximum(bad, jnp.max(fine, axis=0, keepdims=True))
        low = data[0] * pl.reciprocal(total[0], approx=True)
        high = data[1] * pl.reciprocal(total[1], approx=True)
        outs.append(jnp.concatenate([low, high[:, : width - 128]], axis=1).astype(bf16))
    return jnp.concatenate(outs, axis=0), bad


def window_blocks(windows, masks, weights, safe):
    attn_gain, qkv, out_w, mlp_gain, up_w, down_w = weights
    width = windows[0].shape[-1]
    chunk = 128 if safe else 256
    outs = []
    bad = jnp.zeros((1, 128), f32)

    def feed_forward(resid, normed):
        activ = dot_f32(normed, up_w)
        activ = (0.5 * activ * (1.0 + lax.erf(activ * f32(0.5**0.5)))).astype(bf16)
        return (resid + dot_f32(activ, down_w)).astype(bf16)

    normed = layer_norm(windows[0], attn_gain).astype(bf16)
    waiting = None
    for i, window in enumerate(windows):
        following = None
        if i + 1 < len(windows):
            following = layer_norm(windows[i + 1], attn_gain).astype(bf16)
        attended, bad_here = attention(
            normed, qkv, width, None if masks is None else masks[i], chunk, safe
        )
        bad = jnp.maximum(bad, bad_here)
        if waiting is not None:
            outs.append(feed_forward(*waiting))
        resid = (window + dot_f32(attended, out_w)).astype(bf16).astype(f32)
        waiting = (resid, layer_norm(resid, mlp_gain).astype(bf16))
        normed = following
    outs.append(feed_forward(*waiting))
    return outs, bad


def prepare(qkv_ref, down_ref, qkv_s, down_s):
    qkv = qkv_ref[...]
    width = qkv.shape[0]
    gap = jnp.zeros((width, 256 - width), bf16)
    parts = []
    for i in range(3):
        parts += [qkv[:, i * width : (i + 1) * width], gap]
    qkv_s[...] = jnp.concatenate(parts, axis=1)
    down_s[...] = down_ref[...].T


def first_kernel(layer, n_extra, x_ref, ag_ref, qkv_ref, out_ref, mg_ref, up_ref, down_ref, *rest):
    *outs_ref, qkv_s, down_s = rest[n_extra:]
    width = x_ref.shape[-1]
    prepare(qkv_ref, down_ref, qkv_s, down_s)
    row = lax.broadcasted_iota(jnp.int32, (1, WIN, 1), 1)

    def run(step, safe):
        x = x_ref[...].astype(f32).reshape(WIN * WIN, 2, WIN, width)
        windows = [x[:, i].reshape(TOKENS, width) for i in range(2)]
        weights = (
            ag_ref[layer : layer + 1],
            qkv_s[...],
            out_ref[...],
            mg_ref[layer : layer + 1],
            up_ref[...],
            down_s[...],
        )
        outs, bad = window_blocks(windows, None, weights, safe)
        outs = [out.astype(f32).reshape(WIN * WIN, 1, WIN, width) for out in outs]
        y = jnp.concatenate(outs, axis=1).reshape(WIN, WIN, PAIR, width)
        edge = outs[0].reshape(WIN, 2, 2, 2, WIN, width)
        near = edge[:, :, 0].reshape(-1, WIN, width)
        far = pltpu.roll(edge[:, :, 1].reshape(-1, WIN, width), HALF, 1)
        edge = jnp.where(row < HALF, near, far).reshape(WIN, HALF, WIN, width)
        late, early = slice(HALF, WIN), slice(HALF)
        for ref, value in zip(
            outs_ref, (y[late], y[early], y[late, early], y[early, early], edge[late], edge[early])
        ):
            ref[...] = value.astype(bf16)
        return bad

    run_all(1, run)


def run_all(n_steps, run):
    def body(step, bad):
        return jnp.maximum(bad, run(step, False))

    bad = jnp.zeros((1, 128), f32)
    bad = run(0, False) if n_steps == 1 else lax.fori_loop(0, n_steps, body, bad)

    @pl.when(jnp.max(bad) > 0)
    def _():
        @pl.loop(0, n_steps)
        def _(step):
            run(step, True)


def cost(n_windows, width, args):
    mult = sum(a.shape[1] * a.shape[2] for a in args if a.ndim == 3) + 2 * TOKENS * width
    return pl.CostEstimate(
        flops=16 * n_windows * TOKENS * mult,
        bytes_accessed=4 * n_windows * TOKENS * width,
        transcendentals=n_windows * TOKENS * TOKENS * HEADS,
    )


def weight_specs(layer, args, grid_rank):
    attn_gain, qkv, out_w, mlp_gain, up_w, down_t = args

    def whole(a):
        return pl.BlockSpec(a.shape, lambda *_: (0,) * a.ndim)

    def one(a):
        return pl.BlockSpec((None, *a.shape[1:]), lambda *_: (layer,) + (0,) * (a.ndim - 1))

    return [whole(attn_gain), one(qkv), one(out_w), whole(mlp_gain), one(up_w), one(down_t)]


def weight_scratch(args):
    _, qkv, _, _, _, down_t = args
    return [
        pltpu.VMEM((qkv.shape[1], 768), bf16),
        pltpu.VMEM((down_t.shape[2], down_t.shape[1]), bf16),
    ]


def whole_spec(shape):
    return pl.BlockSpec(shape, lambda *_: (0,) * len(shape))


def first_block(tokens, args, pair, row, extra, vmem):
    ra, _, _, width = tokens.shape
    shapes = [(HALF, WIN, PAIR, width)] * 2 + [(HALF, HALF, PAIR, width)] * 2
    shapes += [(HALF, HALF, WIN, width)] * 2
    return pl.pallas_call(
        functools.partial(first_kernel, 0, len(extra)),
        grid=(1,),
        in_specs=[
            pl.BlockSpec((ra, WIN, PAIR, width), lambda *_: (0, row, pair, 0)),
            *weight_specs(0, args, 1),
            *[pl.BlockSpec(memory_space=pl.ANY) for _ in extra],
        ],
        out_specs=[whole_spec(shape) for shape in shapes],
        out_shape=[jax.ShapeDtypeStruct(shape, bf16) for shape in shapes],
        scratch_shapes=weight_scratch(args),
        compiler_params=pltpu.CompilerParams(vmem_limit_bytes=vmem),
        cost_estimate=cost(2, width, args),
    )(tokens, *args, *extra)


def second_kernel(layer, columns, n_freq, n_dec, n_pairs, with_edge, n_done, *refs):
    take = iter(refs)
    pairs = [[[next(take) for _ in range(4)] for _ in range(n_dec)] for _ in range(n_pairs)]
    edges = [[next(take) for _ in range(4)] for _ in range(n_dec)] if with_edge else None
    ag_ref, qkv_ref, out_ref, mg_ref, up_ref, down_ref = [next(take) for _ in range(6)]
    merging = n_done > 0
    if merging:
        done_ref, gain_ref, merge_ref = [next(take) for _ in range(3)]
        g_ref = next(take)
    else:
        y_ref = next(take)
    qkv_s, down_s, xs, query_s, key_s = [next(take) for _ in range(5)]
    dec, width = n_dec * WIN, pairs[0][0][0].shape[-1]
    prepare(qkv_ref, down_ref, qkv_s, down_s)
    query_cols, key_cols = split_mask(TOKENS, width)
    query_s[...] = query_cols
    key_s[...] = key_cols
    row = lax.broadcasted_iota(jnp.int32, (1, 1, WIN, 1), 2)
    first_column = columns[0]
    first_pair = first_column // 2 if with_edge else 0

    for i in range(n_dec):
        for late_ra in range(2):
            for late_dec in range(2):
                here = i + late_dec
                pick = late_ra if here < n_dec else 2 + late_ra
                here = here % n_dec
                first = HALF * (1 - late_dec)
                parts = []
                for pair in pairs:
                    body = pair[here][pick][:, first : first + HALF].astype(f32)
                    parts += [body[:, :, :WIN], body[:, :, WIN:]]
                if with_edge:
                    end = edges[here][pick][:, first // 2 : first // 2 + 2].astype(f32)
                    end = end.reshape(-1, WIN, width)
                    end = [
                        part.reshape(HALF, 2, WIN, width)
                        for part in (end, pltpu.roll(end, HALF, 1))
                    ]
                    parts.append(jnp.concatenate(end, axis=1))
                for j in columns:
                    tile = jnp.where(row < HALF, parts[j + 1], parts[j])
                    xs[
                        j - first_column,
                        i,
                        HALF * late_ra : HALF * late_ra + HALF,
                        HALF * late_dec : HALF * late_dec + HALF,
                    ] = tile

    last_ra = (lax.axis_index("ra") == lax.axis_size("ra") - 1).astype(jnp.int32)
    last_dec = (lax.axis_index("dec") == lax.axis_size("dec") - 1).astype(jnp.int32)
    last_freq = (lax.axis_index("freq") == lax.axis_size("freq") - 1).astype(jnp.int32)
    lane = lax.broadcasted_iota(jnp.int32, (1, 128), 1) - (width - 128)

    def keep(out, i, j):
        out = out.reshape(WIN, HALF, 2, WIN, width)
        after = jnp.where(j == n_freq - 1, 0, j + 1)
        for v in range(2):
            for lanes, low in ((slice(128), 0), (slice(width - 128), 128)):
                kept = out[:, :, v, :, low : low + 128]
                place = (low // 128, v, slice(None), slice(i * HALF, i * HALF + HALF))
                z[(*place, after, slice(HALF), lanes)] = kept[:, :, :HALF]
                z[(*place, j, slice(HALF, WIN), lanes)] = kept[:, :, HALF:]

    def run(step, safe):
        weights = (
            ag_ref[layer : layer + 1],
            qkv_s[...],
            out_ref[...],
            mg_ref[layer : layer + 1],
            up_ref[...],
            down_s[...],
        )
        j = first_column + step
        on_freq = jnp.where(j == n_freq - 1, last_freq, 0)
        windows, masks = [], []
        for i in range(n_dec):
            windows.append(xs[step, i].reshape(TOKENS, width))
            on_dec = last_dec if i == n_dec - 1 else 0
            on = jnp.where(lane < 2, last_ra, jnp.where(lane < 4, on_dec, on_freq))
            masks.append((query_s[...], key_s[...], on.astype(f32)))
        outs, bad = window_blocks(windows, masks, weights, safe)
        for i in range(n_dec):
            if merging:
                keep(outs[i].astype(f32), i, j)
            else:
                y_ref[step, i] = outs[i]
        return bad

    if merging:
        z = next(take)
        for j in range(n_done):
            for i in range(n_dec):
                keep(done_ref[j, i].astype(f32), i, j)
    run_all(len(columns), run)
    if not merging:
        return

    out_ra, out_dec, out_freq = WIN // 2, dec // 2, n_freq * HALF
    lines = z.shape[1] * z.shape[2] * z.shape[3] * n_freq * WIN
    flat = z.reshape(2 * lines, 128)
    groups = []
    for w in range(2):
        low = flat[pl.ds(w, lines // 2, stride=2), :]
        high = flat[pl.ds(lines + w, lines // 2, stride=2), :]
        picked = jnp.concatenate([low, high[:, : width - 128]], axis=1)
        groups.append(picked.reshape(2, out_ra, 2, out_dec * out_freq, width))
    merge_in = [
        groups[w][v, :, u].reshape(-1, width) for u in range(2) for v in range(2) for w in range(2)
    ]
    total = merge_in[0]
    for part in merge_in[1:]:
        total = total + part
    mean = jnp.sum(total, axis=-1, keepdims=True) * f32(1 / (8 * width))
    centred = [part - mean for part in merge_in]
    total = centred[0] * centred[0]
    for part in centred[1:]:
        total = total + part * part
    scale = lax.rsqrt(jnp.sum(total, axis=-1, keepdims=True) * f32(1 / (8 * width)) + 1e-05)
    merged = None
    for n, part in enumerate(centred):
        normed = (part * scale * gain_ref[n : n + 1]).astype(bf16)
        term = dot_f32(normed, merge_ref[n * width : (n + 1) * width])
        merged = term if merged is None else merged + term
    merged = merged.reshape(out_ra, out_dec, out_freq, -1)
    g_ref[...] = merged.astype(bf16)


def second_block(columns, n_freq, n_dec, pairs, edges, args, merge=None):
    width = pairs[0][0][0].shape[-1]
    dec = n_dec * WIN
    groups = pairs + ([edges] if edges else [])
    inputs = [part for group in groups for parts in group for part in parts]
    specs = [whole_spec(p.shape) for p in inputs] + weight_specs(1, args, 1)
    inputs += args
    scratch = [
        *weight_scratch(args),
        pltpu.VMEM((len(columns), n_dec, WIN, WIN, WIN, width), f32),
        pltpu.VMEM((TOKENS, 128), f32),
        pltpu.VMEM((TOKENS, 128), f32),
    ]
    n_done = 0
    if merge is None:
        shapes = [(len(columns), n_dec, TOKENS, width)]
    else:
        done, gain, merge_weight = merge
        n_done = done.shape[0]
        extra = [done, gain.reshape(8, width), merge_weight]
        inputs += extra
        specs += [whole_spec(e.shape) for e in extra]
        shapes = [(HALF, dec // 2, n_freq * HALF, merge_weight.shape[1])]
        scratch.append(pltpu.VMEM((2, 2, WIN, dec // 2, n_freq, WIN, 128), f32))
    return pl.pallas_call(
        functools.partial(
            second_kernel, 1, columns, n_freq, n_dec, len(pairs), edges is not None, n_done
        ),
        grid=(1,),
        in_specs=specs,
        out_specs=[whole_spec(shape) for shape in shapes],
        out_shape=[jax.ShapeDtypeStruct(shape, bf16) for shape in shapes],
        scratch_shapes=scratch,
        compiler_params=pltpu.CompilerParams(vmem_limit_bytes=VMEM_LIMIT),
        cost_estimate=cost(len(columns) * n_dec, width, args),
    )(*inputs)


def send(value, steps):
    axes = tuple(steps)
    sizes = [lax.axis_size(axis) for axis in axes]
    total = 1
    for size in sizes:
        total *= size
    pairs = []
    for source in range(total):
        rest, coords = source, []
        for size in reversed(sizes):
            coords.insert(0, rest % size)
            rest //= size
        target = 0
        for axis, size, coord in zip(axes, sizes, coords):
            target = target * size + (coord - steps[axis]) % size
        pairs.append((source, target))
    return lax.ppermute(value, axes, pairs)


def on_device(
    tokens,
    attn_gain,
    qkv_weight,
    out_weight,
    mlp_gain,
    up_weight,
    down_weight,
    merge_gain,
    merge_weight,
):
    args = (
        attn_gain,
        qkv_weight,
        out_weight,
        mlp_gain,
        up_weight,
        jnp.swapaxes(down_weight, 1, 2),
    )
    n_dec, n_freq = tokens.shape[1] // WIN, tokens.shape[2] // WIN
    to_ra, to_dec, to_freq = {"ra": 1}, {"dec": 1}, {"freq": 1}

    def with_halo(rows):
        out = [[late, send(early, to_ra)] for late, early, *_ in rows]
        late_dec, early_dec = rows[0][2:]
        dec_parts = [send(late_dec, to_dec), send(early_dec, {**to_ra, **to_dec})]
        return [row + dec_parts for row in out]

    pairs, extra = [], []
    for pair in range(n_freq // 2):
        rows = []
        for row in range(n_dec):
            limit = FIRST_LIMIT if pair == row == 0 else VMEM_LIMIT
            wait = extra if row == n_dec - 1 else []
            rows.append(first_block(tokens, args, pair, row, wait, limit))
        pairs.append(with_halo([row[:4] for row in rows]))
        if pair == 0:
            ends = [[send(edge, to_freq) for edge in row[4:]] for row in rows]
            extra = [*pairs[0][0][2:], pairs[0][0][1], *[edge for row in ends for edge in row]]
    late_end, early_end = ends[0]
    edges = with_halo([[*row, late_end[:, :2], early_end[:, :2]] for row in ends])
    (done,) = second_block([0], n_freq, n_dec, pairs[:1], None, args)
    (grid,) = second_block(
        list(range(1, n_freq)), n_freq, n_dec, pairs, edges, args, (done, merge_gain, merge_weight)
    )
    q = HALF // 2
    incoming = send(grid[-q:], {"ra": -1})
    grid = jnp.concatenate([incoming, grid[:-q]], axis=0)
    incoming = send(grid[:, -q:], {"dec": -1})
    grid = jnp.concatenate([incoming, grid[:, :-q]], axis=1)
    incoming = send(grid[:, :, :q], {"freq": -1})
    return jnp.concatenate([incoming, grid[:, :, q:]], axis=2)


def solution(mesh):
    placed = (P("ra", "dec", "freq", None), P(), P(), P(), P(), P(), P(), P(), P())
    return jax.shard_map(
        on_device,
        mesh=mesh,
        in_specs=placed,
        out_specs=P("ra", "dec", "freq", None),
        check_vma=False,
    )
```

time: 412 us -> 244 us (0.59)
  matrix products: 268 us -> 0 us
  Pallas kernels: 0 us -> 197 us
  local copies, waits for them, and re-layouts: 49.6 us -> 7.94 us
  waiting for transfers between devices: 52.7 us -> 12.6 us
  other arithmetic: 27.8 us -> 0.87 us
  starting transfers between devices: 11 us -> 21.1 us
    pallas_call x0 -> x6, Pallas kernels: none -> 197 us  [the longest x2 99.5 us: second_block(): pl.pallas_call(functools.partial(second_kernel, 1, columns, n_freq, n_dec...]
    dot_general x65 -> x0, matrix products: 177 us -> none  [the longest x16 92.5 us: window_block(): jnp.dot(activ, down_mat, preferred_element_type=jnp.float32)]
    sub x16 -> x0, matrix products: 91.2 us -> none  [window_block(): exponent = jnp.exp(scores - row_top)]
    ppermute x6 -> x19, waiting for transfers between devices: 52.7 us -> 12.6 us  [send(): return lax.ppermute(value, axes, pairs)]
    convert_element_type x3 -> x0, local copies, waits for them, and re-layouts: 15.6 us -> none  [merge_patches(): grouped.astype(jnp.float32)]
    while x4 -> x0, local copies, waits for them, and re-layouts: 11.3 us -> none  [the longest x2 5.68 us: run_block(): lax.map(lambda window: window_block(window, None, layer_params), windows)]
    reduce_sum x50 -> x0, other arithmetic: 10.9 us -> none  [the longest x33 6.04 us: layer_norm(): row_var = jnp.mean(centred * centred, axis=-1, keepdims=True)]
    ppermute x6 -> x19, starting transfers between devices: 11 us -> 21.1 us  [send(): return lax.ppermute(value, axes, pairs)]
  transfers between devices with their start and end apart: 6 -> 19, of which waited for: 6 -> 3; matrix products, arithmetic and copies ran while one was open for 2% -> 0% of each run, Pallas kernels for 0% -> 40%
where the time goes in v1:
time: 244 us; the launch traced here: 240 us
  Pallas kernels  197 us (81%)
  starting transfers between devices  21.1 us (9%)
  waiting for transfers between devices  12.6 us (5%)
  local copies, waits for them, and re-layouts  7.94 us (3%)
    pallas_call x2, Pallas kernels, second_block(): pl.pallas_call(functools.partial(second_kernel, 1, columns, n_freq, n_dec...  99.5 us
    pallas_call x4, Pallas kernels, first_block(): pl.pallas_call(functools.partial(first_kernel, 0, len(extra)), grid=(1,),...  97.1 us
    ppermute x19, starting transfers between devices, send(): return lax.ppermute(value, axes, pairs)  21.1 us
    ppermute x19, waiting for transfers between devices, send(): return lax.ppermute(value, axes, pairs)  12.6 us
    unnamed x46, local copies, waits for them, and re-layouts  7.12 us
  transfers between devices with their start and end apart: 19, of which 3 were waited for; matrix products, arithmetic and copies ran while one was open for 0% of the time, Pallas kernels for 40%

profile of v1, /device:TPU:0, one launch (start us, length us, event | category | flops | bytes accessed | tf_op | source)
XLA Modules:
  0.0 239.5 jit_solution(5240718798470230152)
XLA Ops:
  0.0 25.6 %shard_map.91 = (bf16[4,8,16,192]{3,2,1,0:T(8,128)(2,1)}, bf16[4,8,16,192]{3,2,1,0:T(8,128)(2,1)}, bf16[4,4,16,192]{3,2,1,0:T(8,128)(2,1)}, bf16[4,4,16,192]{3,2...) custom-call(bf16[8,16,32,192]{3,2,1,0:T(8,128)(2,1)} %x_ref.7, f32[2,192]{1,0:T(2,128)} %refs_24_.1, ...), custom_call_target="tpu_custom_call" | custom-call | flops 10468982784 | bytes 786432 | tf_op jit(solution)/shard_map/pallas_call | solution.py:235
  25.6 4.5 %collective-permute-start = (bf16[4,8,16,192]{3,2,1,0:T(8,128)(2,1)}, bf16[4,8,16,192]{3,2,1,0:T(8,128)(2,1)}, u32[]{:S(2)}, u32[]{:S(2)}) collective-permute-start(bf16[4,8,16,192]{3,2,1,0:T(8,128)(2,1)} %get-tuple-element.22), channel_id=1, source_target_pairs={{0,28},{4,0},{8,4},{12,8},{16,12},{20,16},{24,20},{28,24},{1,29},{... | collective-permute-start | bytes 589832 | tf_op jit(solution)/shard_map/ppermute | solution.py:433
  30.1 1.5 collective-permute-start.1
  32.4 1.5 collective-permute-start.7
  34.4 0.9 copy-done.9
  35.4 24.0 %shard_map.92 = (bf16[4,8,16,192]{3,2,1,0:T(8,128)(2,1)S(1)}, bf16[4,8,16,192]{3,2,1,0:T(8,128)(2,1)S(1)}, bf16[4,4,16,192]{3,2,1,0:T(8,128)(2,1)}, bf16[4,4,16,...) custom-call(bf16[8,16,32,192]{3,2,1,0:T(8,128)(2,1)S(1)} %copy-done, ...), custom_call_target="tpu_custom_call" | custom-call | flops 10468982784 | bytes 786432 | tf_op jit(solution)/shard_map/pallas_call | solution.py:235
  60.8 1.5 collective-permute-start.10
  62.8 23.7 %shard_map.93 = (bf16[4,8,16,192]{3,2,1,0:T(8,128)(2,1)S(1)}, bf16[4,8,16,192]{3,2,1,0:T(8,128)(2,1)S(1)}, bf16[4,4,16,192]{3,2,1,0:T(8,128)(2,1)S(1)}, bf16[4,4...) custom-call(bf16[8,16,32,192]{3,2,1,0:T(8,128)(2,1)S(1)} %copy-done, ...), custom_call_target="tpu_custom_call" | custom-call | flops 10468982784 | bytes 786432 | tf_op jit(solution)/shard_map/pallas_call | solution.py:235
  89.3 0.8 reshape.3.refs_31_
  90.7 1.5 collective-permute-start.13
  92.2 1.1 collective-permute-start.12
  93.3 1.0 copy-done.5
  94.3 0.9 copy-done.10
  95.3 23.8 %shard_map.94 = (bf16[4,8,16,192]{3,2,1,0:T(8,128)(2,1)S(1)}, bf16[4,8,16,192]{3,2,1,0:T(8,128)(2,1)S(1)}, bf16[4,4,16,192]{3,2,1,0:T(8,128)(2,1)}, bf16[4,4,16,...) custom-call(bf16[8,16,32,192]{3,2,1,0:T(8,128)(2,1)S(1)} %copy-done, ...), custom_call_target="tpu_custom_call" | custom-call | flops 10468982784 | bytes 786432 | tf_op jit(solution)/shard_map/pallas_call | solution.py:235
  119.1 1.6 collective-permute-start.5
  121.3 1.7 collective-permute-start.11
  123.1 24.8 %shard_map.95.refs_30_ = bf16[1,2,512,192]{3,2,1,0:T(8,128)(2,1)S(1)} custom-call(bf16[4,8,16,192]{3,2,1,0:T(8,128)(2,1)S(1)} %copy-done.18, bf16[4,8,16,192]{3,2,1,0:T(8,128)(2,1)} %collective-permute-done.rest_2_.refs_1_, bf16[4,4,16,192]{3,2,1,0:T(8,128)(2,1)S(1)} %collective-permute-done.1.rest_0_.refs_2_.refs_6_, ...), custom_call_target="tpu_custom_call" | custom-call | flops 10468982784 | bytes 786432 | tf_op jit(solution)/shard_map/pallas_call | solution.py:403
  147.9 74.7 %shard_map.96 = bf16[4,8,16,384]{3,2,1,0:T(8,128)(2,1)S(1)} custom-call(bf16[4,8,16,192]{3,2,1,0:T(8,128)(2,1)S(1)} %copy-done.18, bf16[4,8,16,192]{3,2,1,0:T(8,128)(2,1)} %collective-permute-done.rest_2_.refs_1_, bf16[4,4,16,192]{3,2,1,0:T(8,128)(2,1)S(1)} %collective-permute-done.1.rest_0_.refs_2_.refs_6_, ...), custom_call_target="tpu_custom_call" | custom-call | flops 31406948352 | bytes 2359296 | tf_op jit(solution)/shard_map/pallas_call | solution.py:403
  222.7 6.9 %collective-permute-done.16 = bf16[2,8,16,384]{3,2,1,0:T(8,128)(2,1)S(1)} collective-permute-done((bf16[2,8,16,384]{3,2,1,0:T(8,128)(2,1)S(1)}, bf16[2,8,16,384]{3,2,1,0:T(8,128)(2,1)S(1)}, u32[]{:S(2)}, u32[]{:S(2)}) %collective-permute-start.16) | collective-permute-done | bytes 196640 | tf_op jit(solution)/shard_map/ppermute | solution.py:433
  229.6 1.6 collective-permute-start.17
  231.2 3.1 %collective-permute-done.17 = bf16[4,2,16,384]{3,2,1,0:T(8,128)(2,1)S(1)} collective-permute-done((bf16[4,2,16,384]{3,2,1,0:T(8,128)(2,1)S(1)}, bf16[4,2,16,384]{3,2,1,0:T(8,128)(2,1)S(1)}, u32[]{:S(2)}, u32[]{:S(2)}) %collective-permute-start.17) | collective-permute-done | bytes 98336 | tf_op jit(solution)/shard_map/ppermute | solution.py:433
  234.4 1.6 collective-permute-start.18
  235.9 2.6 %collective-permute-done.18 = bf16[4,8,2,384]{3,2,1,0:T(2,128)(2,1)S(1)} collective-permute-done((bf16[4,8,2,384]{3,2,1,0:T(2,128)(2,1)S(1)}, bf16[4,8,2,384]{3,2,1,0:T(2,128)(2,1)S(1)}, u32[]{:S(2)}, u32[]{:S(2)}) %collective-permute-start.18) | collective-permute-done | bytes 49184 | tf_op jit(solution)/shard_map/ppermute | solution.py:433
  238.5 0.8 fusion.4
  (73 shorter events, 7.5 us)
Async XLA Ops:
  0.0 34.4 %copy-start.2 = (bf16[2,192,768]{2,1,0:T(8,128)(2,1)S(1)}, bf16[2,192,768]{2,1,0:T(8,128)(2,1)}, u32[]{:S(2)}) copy-start(bf16[2,192,768]{2,1,0:T(8,128)(2,1)} %refs_28_.1) | copy-start | bytes 1769476
  0.0 34.4 %copy-start.3 = (bf16[2,768,192]{1,2,0:T(8,128)(2,1)S(1)}, bf16[2,768,192]{1,2,0:T(8,128)(2,1)}, u32[]{:S(2)}) copy-start(bf16[2,768,192]{1,2,0:T(8,128)(2,1)} %param.15) | copy-start | bytes 1769476
  0.0 34.4 %copy-start.4 = (bf16[2,192,576]{2,1,0:T(8,128)(2,1)S(1)}, bf16[2,192,576]{2,1,0:T(8,128)(2,1)}, u32[]{:S(2)}) copy-start(bf16[2,192,576]{2,1,0:T(8,128)(2,1)} %refs_25_.1) | copy-start | bytes 1327108
  0.0 34.4 %copy-start.16 = (f32[2,192]{1,0:T(2,128)S(1)}, f32[2,192]{1,0:T(2,128)}, u32[]{:S(2)}) copy-start(f32[2,192]{1,0:T(2,128)} %refs_24_.1) | copy-start | bytes 4612
  0.0 34.4 %copy-start.17 = (f32[2,192]{1,0:T(2,128)S(1)}, f32[2,192]{1,0:T(2,128)}, u32[]{:S(2)}) copy-start(f32[2,192]{1,0:T(2,128)} %refs_27_.1) | copy-start | bytes 4612
  25.6 66.6 %collective-permute-start = (bf16[4,8,16,192]{3,2,1,0:T(8,128)(2,1)}, bf16[4,8,16,192]{3,2,1,0:T(8,128)(2,1)}, u32[]{:S(2)}, u32[]{:S(2)}) collective-permute-start(bf16[4,8,16,192]{3,2,1,0:T(8,128)(2,1)} %get-tuple-element.22), channel_id=1, source_target_pairs={{0,28},{4,0},{8,4},{12,8},{16,12},{20,16},{24,20},{28,24},{1,29},{... | collective-permute-start | bytes 589832 | tf_op jit(solution)/shard_map/ppermute | solution.py:433
  30.1 60.6 %collective-permute-start.1 = (bf16[4,4,16,192]{3,2,1,0:T(8,128)(2,1)}, bf16[4,4,16,192]{3,2,1,0:T(8,128)(2,1)S(1)}, u32[]{:S(2)}, u32[]{:S(2)}) collective-permute-start(bf16[4,4,16,192]{3,2,1,0:T(8,128)(2,1)} %get-tuple-element.23), channel_id=1, source_target_pairs={{0,2},{2,0},{1,3},{3,1},{4,6},{6,4},{5,7},{7,5},{8,10},{10,8},{9,1... | collective-permute-start | bytes 294920 | tf_op jit(solution)/shard_map/ppermute | solution.py:433
  31.7 60.6 %collective-permute-start.2 = (bf16[4,4,16,192]{3,2,1,0:T(8,128)(2,1)}, bf16[4,4,16,192]{3,2,1,0:T(8,128)(2,1)}, u32[]{:S(2)}, u32[]{:S(2)}) collective-permute-start(bf16[4,4,16,192]{3,2,1,0:T(8,128)(2,1)} %get-tuple-element.24), channel_id=1, source_target_pairs={{0,30},{2,28},{4,2},{6,0},{8,6},{10,4},{12,10},{14,8},{16,14},{18,... | collective-permute-start | bytes 294920 | tf_op jit(solution)/shard_map/ppermute | solution.py:433
  32.4 28.4 %collective-permute-start.7 = (bf16[4,4,8,192]{3,2,1,0:T(8,128)(2,1)}, bf16[4,4,8,192]{3,2,1,0:T(8,128)(2,1)S(1)}, u32[]{:S(2)}, u32[]{:S(2)}) collective-permute-start(bf16[4,4,8,192]{3,2,1,0:T(8,128)(2,1)} %get-tuple-element.31), channel_id=1, source_target_pairs={{0,1},{1,0},{2,3},{3,2},{4,5},{5,4},{6,7},{7,6},{8,9},{9,8},{10,11... | collective-permute-start | bytes 147464 | tf_op jit(solution)/shard_map/ppermute | solution.py:433
  33.9 28.4 %collective-permute-start.8 = (bf16[4,4,8,192]{3,2,1,0:T(8,128)(2,1)}, bf16[4,4,8,192]{3,2,1,0:T(8,128)(2,1)S(1)}, u32[]{:S(2)}, u32[]{:S(2)}) collective-permute-start(bf16[4,4,8,192]{3,2,1,0:T(8,128)(2,1)} %get-tuple-element.32), channel_id=1, source_target_pairs={{0,1},{1,0},{2,3},{3,2},{4,5},{5,4},{6,7},{7,6},{8,9},{9,8},{10,11... | collective-permute-start | bytes 147464 | tf_op jit(solution)/shard_map/ppermute | solution.py:433
  60.8 29.3 %collective-permute-start.10 = (bf16[4,4,8,192]{3,2,1,0:T(8,128)(2,1)}, bf16[4,4,8,192]{3,2,1,0:T(8,128)(2,1)}, u32[]{:S(2)}, u32[]{:S(2)}) collective-permute-start(bf16[4,4,8,192]{3,2,1,0:T(8,128)(2,1)} %get-tuple-element.34), channel_id=1, source_target_pairs={{0,1},{1,0},{2,3},{3,2},{4,5},{5,4},{6,7},{7,6},{8,9},{9,8},{10,11... | collective-permute-start | bytes 147464 | tf_op jit(solution)/shard_map/ppermute | solution.py:433
  62.3 27.8 %collective-permute-start.9 = (bf16[4,4,8,192]{3,2,1,0:T(8,128)(2,1)}, bf16[4,4,8,192]{3,2,1,0:T(8,128)(2,1)}, u32[]{:S(2)}, u32[]{:S(2)}) collective-permute-start(bf16[4,4,8,192]{3,2,1,0:T(8,128)(2,1)} %get-tuple-element.33), channel_id=1, source_target_pairs={{0,1},{1,0},{2,3},{3,2},{4,5},{5,4},{6,7},{7,6},{8,9},{9,8},{10,11... | collective-permute-start | bytes 147464 | tf_op jit(solution)/shard_map/ppermute | solution.py:433
  90.1 31.2 %collective-permute-start.3 = (bf16[4,8,16,192]{3,2,1,0:T(8,128)(2,1)}, bf16[4,8,16,192]{3,2,1,0:T(8,128)(2,1)S(1)}, u32[]{:S(2)}, u32[]{:S(2)}) collective-permute-start(bf16[4,8,16,192]{3,2,1,0:T(8,128)(2,1)} %copy-done.7), channel_id=1, source_target_pairs={{0,28},{4,0},{8,4},{12,8},{16,12},{20,16},{24,20},{28,24},{1,29},{... | collective-permute-start | bytes 589832 | tf_op jit(solution)/shard_map/ppermute | solution.py:433
  90.1 57.7 %collective-permute-start.4 = (bf16[4,8,16,192]{3,2,1,0:T(8,128)(2,1)}, bf16[4,8,16,192]{3,2,1,0:T(8,128)(2,1)S(1)}, u32[]{:S(2)}, u32[]{:S(2)}) collective-permute-start(bf16[4,8,16,192]{3,2,1,0:T(8,128)(2,1)} %copy-done.8), channel_id=1, source_target_pairs={{0,28},{4,0},{8,4},{12,8},{16,12},{20,16},{24,20},{28,24},{1,29},{... | collective-permute-start | bytes 589832 | tf_op jit(solution)/shard_map/ppermute | solution.py:433
  90.7 28.4 %collective-permute-start.13 = (bf16[4,2,8,192]{3,2,1,0:T(8,128)(2,1)S(1)}, bf16[4,2,8,192]{3,2,1,0:T(8,128)(2,1)S(1)}, u32[]{:S(2)}, u32[]{:S(2)}) collective-permute-start(bf16[4,2,8,192]{3,2,1,0:T(8,128)(2,1)S(1)} %slice.32), channel_id=1, source_target_pairs={{0,2},{2,0},{1,3},{3,1},{4,6},{6,4},{5,7},{7,5},{8,10},{10,8},{9,1... | collective-permute-start | bytes 73736 | tf_op jit(solution)/shard_map/ppermute | solution.py:433
  92.2 28.5 %collective-permute-start.14 = (bf16[4,2,8,192]{3,2,1,0:T(8,128)(2,1)S(1)}, bf16[4,2,8,192]{3,2,1,0:T(8,128)(2,1)S(1)}, u32[]{:S(2)}, u32[]{:S(2)}) collective-permute-start(bf16[4,2,8,192]{3,2,1,0:T(8,128)(2,1)S(1)} %slice.33), channel_id=1, source_target_pairs={{0,30},{2,28},{4,2},{6,0},{8,6},{10,4},{12,10},{14,8},{16,14},{18,... | collective-permute-start | bytes 73736 | tf_op jit(solution)/shard_map/ppermute | solution.py:433
  92.2 28.5 %collective-permute-start.12 = (bf16[4,4,8,192]{3,2,1,0:T(8,128)(2,1)S(1)}, bf16[4,4,8,192]{3,2,1,0:T(8,128)(2,1)S(1)}, u32[]{:S(2)}, u32[]{:S(2)}) collective-permute-start(bf16[4,4,8,192]{3,2,1,0:T(8,128)(2,1)S(1)} %collective-permute-done.8.rest_4_), channel_id=1, source_target_pairs={{0,28},{4,0},{8,4},{12,8},{16,12},{20,16},{24,20},{28,24},{1,29},{... | collective-permute-start | bytes 147464 | tf_op jit(solution)/shard_map/ppermute | solution.py:433
  119.1 28.7 %collective-permute-start.5 = (bf16[4,4,16,192]{3,2,1,0:T(8,128)(2,1)S(1)}, bf16[4,4,16,192]{3,2,1,0:T(8,128)(2,1)S(1)}, u32[]{:S(2)}, u32[]{:S(2)}) collective-permute-start(bf16[4,4,16,192]{3,2,1,0:T(8,128)(2,1)S(1)} %copy-done.15), channel_id=1, source_target_pairs={{0,2},{2,0},{1,3},{3,1},{4,6},{6,4},{5,7},{7,5},{8,10},{10,8},{9,1... | collective-permute-start | bytes 294920 | tf_op jit(solution)/shard_map/ppermute | solution.py:433
  120.7 27.2 %collective-permute-start.6 = (bf16[4,4,16,192]{3,2,1,0:T(8,128)(2,1)S(1)}, bf16[4,4,16,192]{3,2,1,0:T(8,128)(2,1)S(1)}, u32[]{:S(2)}, u32[]{:S(2)}) collective-permute-start(bf16[4,4,16,192]{3,2,1,0:T(8,128)(2,1)S(1)} %copy-done.13), channel_id=1, source_target_pairs={{0,30},{2,28},{4,2},{6,0},{8,6},{10,4},{12,10},{14,8},{16,14},{18,... | collective-permute-start | bytes 294920 | tf_op jit(solution)/shard_map/ppermute | solution.py:433
  120.7 27.1 %collective-permute-start.15 = (bf16[4,4,8,192]{3,2,1,0:T(8,128)(2,1)}, bf16[4,4,8,192]{3,2,1,0:T(8,128)(2,1)S(1)}, u32[]{:S(2)}, u32[]{:S(2)}) collective-permute-start(bf16[4,4,8,192]{3,2,1,0:T(8,128)(2,1)} %collective-permute-done.10.rest_6_), channel_id=1, source_target_pairs={{0,28},{4,0},{8,4},{12,8},{16,12},{20,16},{24,20},{28,24},{1,29},{... | collective-permute-start | bytes 147464 | tf_op jit(solution)/shard_map/ppermute | solution.py:433
  121.3 26.6 %collective-permute-start.11 = (bf16[4,8,16,192]{3,2,1,0:T(8,128)(2,1)S(1)}, bf16[4,8,16,192]{3,2,1,0:T(8,128)(2,1)S(1)}, u32[]{:S(2)}, u32[]{:S(2)}) collective-permute-start(bf16[4,8,16,192]{3,2,1,0:T(8,128)(2,1)S(1)} %get-tuple-element.36), channel_id=1, source_target_pairs={{0,28},{4,0},{8,4},{12,8},{16,12},{20,16},{24,20},{28,24},{1,29},{... | collective-permute-start | bytes 589832 | tf_op jit(solution)/shard_map/ppermute | solution.py:433
  222.7 6.9 %collective-permute-start.16 = (bf16[2,8,16,384]{3,2,1,0:T(8,128)(2,1)S(1)}, bf16[2,8,16,384]{3,2,1,0:T(8,128)(2,1)S(1)}, u32[]{:S(2)}, u32[]{:S(2)}) collective-permute-start(bf16[2,8,16,384]{3,2,1,0:T(8,128)(2,1)S(1)} %get-tuple-element.37), channel_id=1, source_target_pairs={{0,4},{4,8},{8,12},{12,16},{16,20},{20,24},{24,28},{28,0},{1,5},{5... | collective-permute-start | bytes 589832 | tf_op jit(solution)/shard_map/ppermute | solution.py:433
  229.6 4.7 %collective-permute-start.17 = (bf16[4,2,16,384]{3,2,1,0:T(8,128)(2,1)S(1)}, bf16[4,2,16,384]{3,2,1,0:T(8,128)(2,1)S(1)}, u32[]{:S(2)}, u32[]{:S(2)}) collective-permute-start(bf16[4,2,16,384]{3,2,1,0:T(8,128)(2,1)S(1)} %pad_maximum_fusion), channel_id=1, source_target_pairs={{0,2},{2,0},{1,3},{3,1},{4,6},{6,4},{5,7},{7,5},{8,10},{10,8},{9,1... | collective-permute-start | bytes 294920 | tf_op jit(solution)/shard_map/ppermute | solution.py:433
  234.4 4.2 %collective-permute-start.18 = (bf16[4,8,2,384]{3,2,1,0:T(2,128)(2,1)S(1)}, bf16[4,8,2,384]{3,2,1,0:T(2,128)(2,1)S(1)}, u32[]{:S(2)}, u32[]{:S(2)}) collective-permute-start(bf16[4,8,2,384]{3,2,1,0:T(2,128)(2,1)S(1)} %pad_maximum_fusion.1), channel_id=1, source_target_pairs={{0,1},{1,0},{2,3},{3,2},{4,5},{5,4},{6,7},{7,6},{8,9},{9,8},{10,11... | collective-permute-start | bytes 147464 | tf_op jit(solution)/shard_map/ppermute | solution.py:433
  (18 other events, 251.5 us)
